TPU v7x, 32 devices: a whole 2x2x4 slice. The times are simulated.
32 devices in a mesh: strip: 8 (over z, y), sub: 4 (over x, core).
Axes of the slice: x: 2, y: 2, z: 4, core: 2. Of those that a mesh axis runs over, the one named last changes fastest.
Arguments:
- currents: bfloat16 [32, 64, 32, 128], P('strip', 'sub'), may hold values from -6 to 6
- near_blocks: bfloat16 [32, 64, 9, 1024], P('strip', 'sub'), may hold values from -0.375 to 0.375
- near_index: int32 [32, 64, 9], P('strip', 'sub'), may hold values from -1 to 2047, as said below
- box_of_patch: int32 [32, 64], P('strip', 'sub'), may hold values from 0 to 255, as said below
- box_centre: float32 [256, 2], P(('strip', 'sub')), as said below
- patch_angle: float32 [32, 64, 128], P('strip', 'sub'), may hold values from -3.140625 to 3.140625
- aggregation: bfloat16 [2, 128, 32], replicated, may hold values from -1 to 1
- disaggregation: bfloat16 [2, 128, 32], replicated, may hold values from -0.375 to 0.375
- strip_shift: float32 [8, 2, 128], P('strip'), may hold values from -1 to 1, as said below
Outputs:
- operator_image: bfloat16 [32, 64, 32, 128], P('strip', 'sub')
Inputs may be any that keep to these rules, and one draw needn't show every extreme that they name: `near_index`: each patch's list holds ids of distinct patches that lie within one row and one column of it, the patch itself always among them, listed entries first and -1 in the remaining slots; some lists are full. `box_of_patch`: the patches of device block (i, j), rows i * 4 to (i + 1) * 4 - 1 and columns j * 16 to (j + 1) * 16 - 1, name only boxes (i * 4 + j) * 8 to (i * 4 + j + 1) * 8 - 1, each exactly 8 times. `box_centre`: box b with b // 8 = i * 4 + j has its centre in [i * 4, (i + 1) * 4] x [j * 16, (j + 1) * 16]. `strip_shift`: every translation has magnitude at most 1.
All inputs are finite; a program needn't handle non-finite values.
Results may differ from a plain program's by a relative error of at most 0.009.
Values may be sent and summed in bfloat16 or wider, within the bound.
A program may use at most 128 MiB of HBM per device.

v0:
```python
import functools
import math

import jax
import jax.numpy as jnp
from jax import lax
from jax.experimental import pallas as pl
from jax.experimental.pallas import tpu as pltpu
from jax.sharding import PartitionSpec as P

wave_number = 1.5
strip_weight = 0.03
MESH = pl.DeviceIdType.MESH
f32 = jnp.float32
bf16 = jnp.bfloat16


def gather_boxes(perm_ref, cur_ref, angle_ref, agg_ref, box_ref, cos_ref, sin_ref, x_ref, e_ref):
    n_sub, n_box, _, quarter, _ = box_ref.shape
    n_patch, n_dirs = angle_ref.shape
    n_units = cur_ref.shape[1]
    per_box = n_patch // n_box
    cos_ref[...] = jnp.cos(angle_ref[...])
    sin_ref[...] = jnp.sin(angle_ref[...])

    def one_box(b, carry):
        agg_re, agg_im = agg_ref[0], agg_ref[1]
        for i in range(per_box):
            p = perm_ref[b * per_box + i]
            rows = slice(i * n_units, (i + 1) * n_units)
            x_ref[rows, :] = cur_ref[p]
            c = cos_ref[pl.ds(p, 1), :]
            s = sin_ref[pl.ds(p, 1), :]
            e_ref[rows, 0:n_dirs] = (c * agg_re - s * agg_im).astype(bf16)
            e_ref[rows, n_dirs : 2 * n_dirs] = (s * agg_re + c * agg_im).astype(bf16)
        values = lax.dot_general(
            e_ref[...], x_ref[...], (((0,), (0,)), ((), ())), preferred_element_type=f32
        ).astype(bf16)
        for c in range(2):
            for q in range(n_sub):
                at = c * n_dirs + q * quarter
                box_ref[q, b, c] = values[at : at + quarter]
        return carry

    lax.fori_loop(0, n_box, one_box, 0)


def near_part(located_ref, nb_ref, pad_ref, near_ref, a_ref, x_ref):
    n_patch, n_slots, _ = nb_ref.shape
    n_units, n_sides = near_ref.shape[1:]
    lanes = lax.broadcasted_iota(jnp.int32, (8, 128), 1) // 32

    def pick(parts):
        out = parts[0]
        for i in range(1, 4):
            out = jnp.where(lanes == i, parts[i], out)
        return out

    def one_patch(p, carry):
        for q in range(8):
            a_ref[q * 16 : q * 16 + n_slots, :] = nb_ref[p, :, q * 128 : (q + 1) * 128].astype(f32)
        for j in range(n_slots):
            x_ref[j * n_units : (j + 1) * n_units, :] = pad_ref[located_ref[p * n_slots + j]]
        flat = [a_ref[pl.ds(j, 8, stride=16), :] for j in range(n_slots)]
        lhs = []
        for g in range(2):
            group = flat[g * 4 : g * 4 + 4]
            rolled = []
            for d in range(4):
                mixed = pick([group[(u + d) % 4] for u in range(4)])
                rolled.append(mixed if d == 0 else pltpu.roll(mixed, 32 * d, 1))
            lhs.append(
                jnp.concatenate([pick([rolled[(j - u) % 4] for j in range(4)]) for u in range(4)], axis=0)
            )
        last = jnp.concatenate(
            [flat[8]] + [pltpu.roll(flat[8], 128 - 32 * u, 1) for u in range(1, 4)], axis=0
        )
        total = jnp.dot(
            jnp.concatenate(lhs, axis=1).astype(bf16), x_ref[0:256, :], preferred_element_type=f32
        )
        total += jnp.dot(
            last[:, 0:n_units].astype(bf16), x_ref[256 : 256 + n_units, :], preferred_element_type=f32
        )
        for u in range(4):
            near_ref[p, pl.ds(u, 8, stride=4), :] = total[u * 8 : u * 8 + 8]
        return carry

    lax.fori_loop(0, n_patch, one_patch, 0)


def far_part(perm_ref, slot_ref, lf_ref, dis_ref, cos_ref, sin_ref, near_ref, out_ref, d_ref, far_ref):
    n_sub, n_box, _, quarter, n_sides = lf_ref.shape
    n_patch, n_dirs = cos_ref.shape
    n_units = near_ref.shape[1]
    per_box = n_patch // n_box

    def one_box(b, carry):
        dis_re, dis_im = dis_ref[0], dis_ref[1]
        for i in range(per_box):
            p = perm_ref[b * per_box + i]
            rows = slice(i * n_units, (i + 1) * n_units)
            c = cos_ref[pl.ds(p, 1), :]
            s = sin_ref[pl.ds(p, 1), :]
            d_ref[rows, 0:n_dirs] = (c * dis_re - s * dis_im).astype(bf16)
            d_ref[rows, n_dirs : 2 * n_dirs] = (s * dis_re + c * dis_im).astype(bf16)
        field = jnp.concatenate([lf_ref[q, b, c] for c in range(2) for q in range(n_sub)], axis=0)
        far = jnp.dot(d_ref[...], field, preferred_element_type=f32)
        for i in range(per_box):
            far_ref[b * per_box + i] = far[i * n_units : (i + 1) * n_units]
        return carry

    lax.fori_loop(0, n_box, one_box, 0)

    def one_patch(p, carry):
        out_ref[p] = (near_ref[p] + far_ref[slot_ref[p]]).astype(bf16)
        return carry

    lax.fori_loop(0, n_patch, one_patch, 0)


def fused(
    n_strip, n_sub,
    perm_ref, slot_ref, located_ref, cur_ref, nb_ref, angle_ref, agg_ref, dis_ref, centre_ref, shift_ref,
    out_ref,
    pad_ref, box_ref, cos_ref, sin_ref, x_ref, e_ref, near_ref, a_ref, far_ref, lf_ref,
    cen_ref, shf_ref, in_ref, wide_ref, w_ref, inc_ref, exp_ref, coef_ref, send_ref,
    halo_send, halo_recv, cen_send, cen_recv, shf_send, shf_recv, a2a_send, a2a_recv,
    exp_send, exp_recv, back_send, back_recv,
):
    strip = lax.axis_index("strip")
    sub = lax.axis_index("sub")
    rows_x, rows_y = 4, 16
    rows_x, rows_y = cur_ref.shape[0], cur_ref.shape[1]
    n_units, n_sides = cur_ref.shape[2], cur_ref.shape[3]
    n_patch = rows_x * rows_y
    n_dirs = angle_ref.shape[1]
    quarter = n_dirs // n_sub
    n_box = centre_ref.shape[0]
    all_box = n_box * n_sub
    wide_y = rows_y + 2

    def sub_peer(d):
        return lax.rem(sub + d, n_sub)

    def strip_peer(d):
        return lax.rem(strip + d, n_strip)

    offsets = [(dx, dy) for dx in (-1, 0, 1) for dy in (-1, 0, 1) if dx or dy]

    barrier = pltpu.get_barrier_semaphore()
    for dx in (-1, 1):
        for dy in (-1, 1):
            pl.semaphore_signal(
                barrier, inc=1, device_id=(strip_peer(dx + n_strip), sub_peer(dy + n_sub)), device_id_type=MESH
            )
    for d in range(1, n_sub):
        pl.semaphore_signal(barrier, inc=1, device_id=(strip, sub_peer(d)), device_id_type=MESH)

    def greet(d, carry):
        pl.semaphore_signal(barrier, inc=1, device_id=(strip_peer(d), sub), device_id_type=MESH)
        return carry

    lax.fori_loop(1, n_strip, greet, 0)

    cen_ref[sub] = jnp.zeros((n_box, 128), f32)
    cen_ref[sub, :, 0:2] = centre_ref[...]
    shf_ref[strip] = jnp.zeros((8, n_dirs), f32)
    shf_ref[strip, 0:2, :] = shift_ref[0]
    pl.semaphore_wait(barrier, 4 + n_sub - 1 + n_strip - 1)

    def cen_copy(d):
        return pltpu.make_async_remote_copy(
            src_ref=cen_ref.at[sub], dst_ref=cen_ref.at[sub],
            send_sem=cen_send.at[d], recv_sem=cen_recv.at[d],
            device_id=(strip, sub_peer(d)), device_id_type=MESH,
        )

    def cen_wait(d):
        src = lax.rem(sub + n_sub - d, n_sub)
        return pltpu.make_async_remote_copy(
            src_ref=cen_ref.at[src], dst_ref=cen_ref.at[src],
            send_sem=cen_send.at[d], recv_sem=cen_recv.at[d],
            device_id=(strip, sub_peer(d)), device_id_type=MESH,
        )

    def strip_copy(buf, send, recv, d, at):
        return pltpu.make_async_remote_copy(
            src_ref=buf.at[at], dst_ref=buf.at[at],
            send_sem=send.at[d], recv_sem=recv.at[d],
            device_id=(strip_peer(d), sub), device_id_type=MESH,
        )

    def halo_copy(n):
        dx, dy = offsets[n]
        src_x = {-1: slice(0, 1), 0: slice(0, rows_x), 1: slice(rows_x - 1, rows_x)}[dx]
        src_y = {-1: slice(0, 1), 0: slice(0, rows_y), 1: slice(rows_y - 1, rows_y)}[dy]
        dst_x = {-1: slice(rows_x + 1, rows_x + 2), 0: slice(1, rows_x + 1), 1: slice(0, 1)}[dx]
        dst_y = {-1: slice(rows_y + 1, rows_y + 2), 0: slice(1, rows_y + 1), 1: slice(0, 1)}[dy]
        return pltpu.make_async_remote_copy(
            src_ref=cur_ref.at[src_x, src_y], dst_ref=pad_ref.at[dst_x, dst_y],
            send_sem=halo_send.at[n], recv_sem=halo_recv.at[n],
            device_id=(strip_peer(dx + n_strip), sub_peer(dy + n_sub)), device_id_type=MESH,
        )

    for d in range(1, n_sub):
        cen_copy(d).start()

    def send_shift(d, carry):
        strip_copy(shf_ref, shf_send, shf_recv, d, strip).start()
        return carry

    lax.fori_loop(1, n_strip, send_shift, 0)
    for n in range(len(offsets)):
        halo_copy(n).start()

    flat_cur = cur_ref.reshape(n_patch, n_units, n_sides)
    flat_pad = pad_ref.reshape((rows_x + 3) * wide_y, n_units, n_sides)

    gather_boxes(perm_ref, flat_cur, angle_ref, agg_ref, box_ref, cos_ref, sin_ref, x_ref.at[0:256], e_ref)

    def a2a_copy(d):
        return pltpu.make_async_remote_copy(
            src_ref=box_ref.at[sub_peer(d)], dst_ref=in_ref.at[d],
            send_sem=a2a_send.at[d], recv_sem=a2a_recv.at[d],
            device_id=(strip, sub_peer(d)), device_id_type=MESH,
        )

    for d in range(1, n_sub):
        a2a_copy(d).start()

    for x in range(rows_x):
        pad_ref[x + 1, 1 : rows_y + 1] = cur_ref[x]
    pad_ref[rows_x + 2, 0] = jnp.zeros((n_units, n_sides), bf16)

    def wait_shift(d, carry):
        src = lax.rem(strip + n_strip - d, n_strip)
        strip_copy(shf_ref, shf_send, shf_recv, d, src).wait_recv()
        return carry

    lax.fori_loop(1, n_strip, wait_shift, 0)
    for d in range(1, n_sub):
        cen_wait(d).wait_recv()
    one = jnp.ones((1, n_dirs), f32)
    zero = jnp.zeros((1, n_dirs), f32)

    def times(a, b):
        return a[0] * b[0] - a[1] * b[1], a[0] * b[1] + a[1] * b[0]

    coef = [None] * n_strip
    run = (one, zero)
    for q in reversed(range(n_strip)):
        t = (shf_ref[q, 0:1, :], shf_ref[q, 1:2, :])
        coef[q] = tuple(jnp.where(q < strip, part, 0.0) for part in run)
        run = times((jnp.where(q <= strip, t[0], 1.0), jnp.where(q <= strip, t[1], 0.0)), run)
    run = (one, zero)
    for q in range(n_strip):
        t = (shf_ref[q, 0:1, :], -shf_ref[q, 1:2, :])
        coef[q] = tuple(a + jnp.where(q > strip, part, 0.0) for a, part in zip(coef[q], run))
        run = times((jnp.where(q >= strip, t[0], 1.0), jnp.where(q >= strip, t[1], 0.0)), run)
    stacked = jnp.concatenate([c[0] for c in coef] + [c[1] for c in coef], axis=0)
    coef_ref[...] = stacked.T
    here = coef_ref[pl.ds(pl.multiple_of(sub * quarter, quarter), quarter), :]

    cen_col = cen_ref[...].reshape(all_box, 128)
    cen_row = cen_col.T
    col_x, col_y = cen_col[:, 0:1], cen_col[:, 1:2]
    row_x, row_y = cen_row[0:1, :], cen_row[1:2, :]
    step = 2.0 * math.pi / n_dirs
    k_col = lax.broadcasted_iota(jnp.int32, (quarter, all_box), 0) + sub * quarter
    angle = k_col.astype(f32) * step
    mid_x = (strip.astype(f32) + 0.5) * rows_x
    mid_y = 0.5 * rows_y * n_sub
    psi = wave_number * ((row_x - mid_x) * jnp.cos(angle) + (row_y - mid_y) * jnp.sin(angle))
    psi_re, psi_im = jnp.cos(psi), jnp.sin(psi)

    fold = 128 // all_box
    dx = col_x - jnp.concatenate([row_x] * fold, axis=1)
    dy = col_y - jnp.concatenate([row_y] * fold, axis=1)
    rho = jnp.sqrt(dx * dx + dy * dy)
    lane = lax.broadcasted_iota(jnp.int32, (all_box, 128), 1)
    target = lax.broadcasted_iota(jnp.int32, (all_box, 128), 0)
    amplitude = jnp.where(lane % all_box != target, 1.0 / (1.0 + rho), 0.0)
    lane_k = lax.broadcasted_iota(jnp.int32, (1, 128), 1) // all_box

    def weights(g, carry):
        turn = (lane_k + g * fold + sub * quarter).astype(f32) * step
        arg = wave_number * (rho + jnp.cos(turn) * dx + jnp.sin(turn) * dy)
        w_re = (amplitude * jnp.cos(arg)).astype(bf16).astype(f32)
        w_im = (amplitude * jnp.sin(arg)).astype(bf16).astype(f32)
        for i in range(fold):
            part = slice(i * all_box, (i + 1) * all_box)
            a, b = w_re[:, part], w_im[:, part]
            w_ref[g * fold + i] = jnp.concatenate(
                [jnp.concatenate([a, -b], axis=1), jnp.concatenate([b, a], axis=1)], axis=0
            ).astype(bf16)
        return carry

    lax.fori_loop(0, quarter // fold, weights, 0)

    def source(d):
        return lax.rem(sub + n_sub - d, n_sub)

    for d in range(n_sub):
        if d:
            a2a_copy(d).wait_recv()
        base = source(d)
        for b in range(n_box):
            for c in range(2):
                block = box_ref[sub, b, c] if d == 0 else in_ref[d, b, c]
                at = (c * all_box + base * n_box + b) * quarter
                wide_ref[pl.ds(pl.multiple_of(at, quarter), quarter), :] = block.astype(f32)

    total_re = jnp.zeros((quarter, n_sides), f32)
    total_im = jnp.zeros((quarter, n_sides), f32)
    for b in range(all_box):
        p_re, p_im = psi_re[:, b : b + 1], psi_im[:, b : b + 1]
        v_re = wide_ref[b * quarter : (b + 1) * quarter, :]
        v_im = wide_ref[(all_box + b) * quarter : (all_box + b + 1) * quarter, :]
        total_re += p_re * v_re - p_im * v_im
        total_im += p_im * v_re + p_re * v_im
    exp_ref[strip, 0] = (strip_weight * total_re).astype(bf16)
    exp_ref[strip, 1] = (strip_weight * total_im).astype(bf16)

    def send_exp(d, carry):
        strip_copy(exp_ref, exp_send, exp_recv, d, strip).start()
        return carry

    lax.fori_loop(1, n_strip, send_exp, 0)

    def interact(k, carry):
        rhs = wide_ref[pl.ds(k, 2 * all_box, stride=quarter), :].astype(bf16)
        inc_ref[pl.ds(k, 2 * all_box, stride=quarter), :] = jnp.dot(
            w_ref[k], rhs, preferred_element_type=f32
        )
        return carry

    lax.fori_loop(0, quarter, interact, 0)

    def wait_exp(d, carry):
        src = lax.rem(strip + n_strip - d, n_strip)
        strip_copy(exp_ref, exp_send, exp_recv, d, src).wait_recv()
        return carry

    lax.fori_loop(1, n_strip, wait_exp, 0)
    field_re = jnp.zeros((quarter, n_sides), f32)
    field_im = jnp.zeros((quarter, n_sides), f32)
    for q in range(n_strip):
        c_re, c_im = here[:, q : q + 1], here[:, n_strip + q : n_strip + q + 1]
        v_re, v_im = exp_ref[q, 0].astype(f32), exp_ref[q, 1].astype(f32)
        field_re += c_re * v_re - c_im * v_im
        field_im += c_re * v_im + c_im * v_re
    for b in range(all_box):
        p_re, p_im = psi_re[:, b : b + 1], psi_im[:, b : b + 1]
        v_re = inc_ref[b * quarter : (b + 1) * quarter, :]
        v_im = inc_ref[(all_box + b) * quarter : (all_box + b + 1) * quarter, :]
        send_ref[b // n_box, b % n_box, 0] = (v_re + p_re * field_re + p_im * field_im).astype(bf16)
        send_ref[b // n_box, b % n_box, 1] = (v_im + p_re * field_im - p_im * field_re).astype(bf16)

    def back_copy(d, at):
        return pltpu.make_async_remote_copy(
            src_ref=send_ref.at[sub_peer(d)], dst_ref=lf_ref.at[at],
            send_sem=back_send.at[d], recv_sem=back_recv.at[d],
            device_id=(strip, sub_peer(d)), device_id_type=MESH,
        )

    for d in range(1, n_sub):
        back_copy(d, sub).start()
    lf_ref[sub] = send_ref[sub]

    for n in range(len(offsets)):
        halo_copy(n).wait_recv()
    near_part(located_ref, nb_ref, flat_pad, near_ref, a_ref, x_ref)

    for d in range(1, n_sub):
        back_copy(d, source(d)).wait_recv()
    far_part(perm_ref, slot_ref, lf_ref, dis_ref, cos_ref, sin_ref, near_ref, out_ref, e_ref, far_ref)

    for d in range(1, n_sub):
        cen_copy(d).wait_send()
        a2a_copy(d).wait_send()
        back_copy(d, sub).wait_send()

    def drain(d, carry):
        strip_copy(shf_ref, shf_send, shf_recv, d, strip).wait_send()
        strip_copy(exp_ref, exp_send, exp_recv, d, strip).wait_send()
        return carry

    lax.fori_loop(1, n_strip, drain, 0)
    for n in range(len(offsets)):
        halo_copy(n).wait_send()


def per_device(
    currents,
    near_blocks,
    near_index,
    box_of_patch,
    box_centre,
    patch_angle,
    aggregation,
    disaggregation,
    strip_shift,
):
    rows_x, rows_y, n_units, n_sides = currents.shape
    n_dirs = patch_angle.shape[2]
    n_slots = near_index.shape[2]
    n_patch = rows_x * rows_y
    box_dev = box_centre.shape[0]
    n_sub = lax.axis_size("sub")
    n_strip = lax.axis_size("strip")
    strip_pos = lax.axis_index("strip")
    sub_pos = lax.axis_index("sub")
    ny_total = rows_y * n_sub
    quarter = n_dirs // n_sub
    all_box = box_dev * n_sub
    wanted = near_index.reshape(n_patch * n_slots)
    located = (wanted // ny_total - strip_pos * rows_x + 1) * (rows_y + 2) + (
        wanted % ny_total - sub_pos * rows_y + 1
    )
    located = jnp.where(wanted >= 0, located, (rows_x + 2) * (rows_y + 2))
    ids = jnp.arange(n_patch, dtype=jnp.int32)
    key = box_of_patch.reshape(n_patch) * n_patch + ids
    slot = jnp.sum((key[None, :] < key[:, None]).astype(jnp.int32), axis=1)
    perm = jnp.sum(jnp.where(slot[None, :] == ids[:, None], ids[None, :], 0), axis=1)
    smem = pl.BlockSpec(memory_space=pltpu.SMEM)
    vmem = pl.BlockSpec(memory_space=pltpu.VMEM)
    dma = pltpu.SemaphoreType.DMA
    scratch = [
        pltpu.VMEM((rows_x + 3, rows_y + 2, n_units, n_sides), bf16),
        pltpu.VMEM((n_sub, box_dev, 2, quarter, n_sides), bf16),
        pltpu.VMEM((n_patch, n_dirs), f32),
        pltpu.VMEM((n_patch, n_dirs), f32),
        pltpu.VMEM((n_slots * n_units, n_sides), bf16),
        pltpu.VMEM((n_patch // box_dev * n_units, 2 * n_dirs), bf16),
        pltpu.VMEM((n_patch, n_units, n_sides), f32),
        pltpu.VMEM((128, 128), f32),
        pltpu.VMEM((n_patch, n_units, n_sides), f32),
        pltpu.VMEM((n_sub, box_dev, 2, quarter, n_sides), bf16),
        pltpu.VMEM((n_sub, box_dev, 128), f32),
        pltpu.VMEM((n_strip, 8, n_dirs), f32),
        pltpu.VMEM((n_sub, box_dev, 2, quarter, n_sides), bf16),
        pltpu.VMEM((2 * all_box * quarter, n_sides), f32),
        pltpu.VMEM((quarter, 2 * all_box, 2 * all_box), bf16),
        pltpu.VMEM((2 * all_box * quarter, n_sides), f32),
        pltpu.VMEM((n_strip, 2, quarter, n_sides), bf16),
        pltpu.VMEM((n_dirs, 2 * n_strip), f32),
        pltpu.VMEM((n_sub, box_dev, 2, quarter, n_sides), bf16),
        dma((8,)), dma((8,)),
        dma((n_sub,)), dma((n_sub,)),
        dma((n_strip,)), dma((n_strip,)),
        dma((n_sub,)), dma((n_sub,)),
        dma((n_strip,)), dma((n_strip,)),
        dma((n_sub,)), dma((n_sub,)),
    ]
    result = pl.pallas_call(
        functools.partial(fused, n_strip, n_sub),
        out_shape=jax.ShapeDtypeStruct((n_patch, n_units, n_sides), bf16),
        in_specs=[smem] * 3 + [vmem] * 7,
        out_specs=vmem,
        scratch_shapes=scratch,
        compiler_params=pltpu.CompilerParams(
            collective_id=0, has_side_effects=True, vmem_limit_bytes=48 * 1024 * 1024
        ),
    )(
        perm,
        slot,
        located,
        currents,
        near_blocks.reshape(n_patch, n_slots, n_units * n_units),
        patch_angle.reshape(n_patch, n_dirs),
        jnp.swapaxes(aggregation, 1, 2).astype(f32),
        jnp.swapaxes(disaggregation, 1, 2).astype(f32),
        box_centre,
        strip_shift,
    )
    return result.reshape(rows_x, rows_y, n_units, n_sides)


def solution(mesh):
    in_specs = (
        P("strip", "sub", None, None),
        P("strip", "sub", None, None),
        P("strip", "sub", None),
        P("strip", "sub"),
        P(("strip", "sub"), None),
        P("strip", "sub", None),
        P(),
        P(),
        P("strip", None, None),
    )
    out_specs = P("strip", "sub", None, None)
    return jax.shard_map(
        per_device, mesh=mesh, in_specs=in_specs, out_specs=out_specs, check_vma=False
    )
```

profile of v0, /device:TPU:1, one launch (start us, length us, event | category | flops | bytes accessed | tf_op | source)
XLA Modules:
  0.0 46.6 jit_solution(3847105106105209932)
XLA Ops:
  0.0 0.0 copy-start.2
  0.0 0.0 copy-start.1
  0.0 0.0 copy-start
  0.0 0.7 %broadcast_multiply_fusion = s32[4,16]{1,0:T(4,128)S(1)} fusion(s32[4,16]{1,0:T(4,128)} %param.12), kind=kLoop, calls=%fused_computation.22 | loop fusion | flops 64 | bytes 512 | tf_op jit(solution)/shard_map/mul | solution.py:422
  0.8 0.1 mul.31
  0.9 0.2 convert_reduce_fusion.slot_ref
  1.0 0.1 select_reduce_fusion.perm_ref
  1.2 0.8 %copy.17.centre_ref = f32[8,2]{1,0:T(8,128)S(1)} copy(f32[8,2]{0,1:T(2,128)} %param.13) | data formatting | bytes 128 | tf_op args[4]
  1.9 0.8 %copy.15 = s32[4,16,9]{2,1,0:T(8,128)S(1)} copy(s32[4,16,9]{1,0,2:T(4,128)} %param.11) | data formatting | bytes 4608 | tf_op args[2]
  2.7 0.1 reshape.34
  2.9 0.7 %convert_bitcast_fusion = (f32[2,32,128]{2,1,0:T(8,128)S(1)}, f32[2,32,128]{2,1,0:T(8,128)S(1)}) fusion(bf16[2,128,32]{1,2,0:T(8,128)(2,1)} %param.16, bf16[2,128,32]{1,2,0:T(8,128)(2,1)} %param.15), kind=kLoop, calls=%fused_computation | loop fusion | flops 16384 | bytes 98304 | tf_op jit(solution)/shard_map/convert_element_type | solution.py:472
  3.6 2.0 %copy.16 = bf16[4,16,9,1024]{3,2,1,0:T(8,128)(2,1)S(1)} copy(bf16[4,16,9,1024]{3,1,2,0:T(8,128)(2,1)} %param.10) | data formatting | bytes 2359296 | tf_op args[1]
  5.7 0.0 copy-done.2
  5.7 0.0 copy-done.1
  5.7 0.0 copy-done
  5.7 40.1 %shard_map.91 = bf16[64,32,128]{2,1,0:T(8,128)(2,1)S(1)} custom-call(s32[64]{0:T(128)S(1)} %select_reduce_fusion.perm_ref, s32[64]{0:T(128)S(1)} %convert_reduce_fusion.slot_ref, s32[576]{0:T(1024)S(1)} %fusion.4.located_ref, bf16[4,16,32,128]{3,2,1,0:T(8,128)(2,1)S(1)} %copy-done, bf16[64,9,1024]{2,1,0:T(8,128)(2,1)S(1)} %bitcast.7, f32[64,128]{1,0:T(8,128)S(1)} %bitcast.9, ...), custom_call_target="tpu_custom_call" | custom-call | tf_op jit(solution)/shard_map/pallas_call | solution.py:455
  45.8 0.8 %copy.19 = bf16[4,16,32,128]{3,2,1,0:T(8,128)(2,1)} copy(bf16[4,16,32,128]{3,2,1,0:T(8,128)(2,1)S(1)} %bitcast.8) | data formatting | bytes 1048576
  (2 shorter events, 0.0 us)
Async XLA Ops:
  0.0 5.7 %copy-start.2 = (f32[1,2,128]{2,1,0:T(2,128)S(1)}, f32[1,2,128]{2,1,0:T(2,128)}, u32[]{:S(2)}) copy-start(f32[1,2,128]{2,1,0:T(2,128)} %shift_ref.1) | copy-start | bytes 3076
  0.0 5.7 %copy-start.1 = (f32[4,16,128]{2,1,0:T(8,128)S(1)}, f32[4,16,128]{2,1,0:T(8,128)}, u32[]{:S(2)}) copy-start(f32[4,16,128]{2,1,0:T(8,128)} %param.14) | copy-start | bytes 98308
  0.0 5.7 %copy-start = (bf16[4,16,32,128]{3,2,1,0:T(8,128)(2,1)S(1)}, bf16[4,16,32,128]{3,2,1,0:T(8,128)(2,1)}, u32[]{:S(2)}) copy-start(bf16[4,16,32,128]{3,2,1,0:T(8,128)(2,1)} %cur_ref.1) | copy-start | bytes 1572868
where the time goes:
time: 47 us; the launch traced here: 46.6 us
  Pallas kernels  40.1 us (85%)
  local copies, waits for them, and re-layouts  4.64 us (10%)
  other arithmetic  1.8 us (4%)
    pallas_call x1, Pallas kernels, per_device(): pl.pallas_call(functools.partial(fused, n_strip, n_sub), out_shape=jax.Sh...  40.1 us
    unnamed x10, local copies, waits for them, and re-layouts  4.42 us

commit v1 on v0

--- a/solution.py
+++ b/solution.py
@@ -10,12 +10,14 @@
 
 wave_number = 1.5
 strip_weight = 0.03
+NSPLIT = 1
+LATER = 2
 MESH = pl.DeviceIdType.MESH
 f32 = jnp.float32
 bf16 = jnp.bfloat16
 
 
-def gather_boxes(perm_ref, cur_ref, angle_ref, agg_ref, box_ref, cos_ref, sin_ref, x_ref, e_ref):
+def gather_boxes(perm_ref, cur_ref, angle_ref, agg_ref, box_ref, cos_ref, sin_ref):
     n_sub, n_box, _, quarter, _ = box_ref.shape
     n_patch, n_dirs = angle_ref.shape
     n_units = cur_ref.shape[1]
@@ -23,30 +25,39 @@
     cos_ref[...] = jnp.cos(angle_ref[...])
     sin_ref[...] = jnp.sin(angle_ref[...])
 
-    def one_box(b, carry):
-        agg_re, agg_im = agg_ref[0], agg_ref[1]
+    agg_re, agg_im = agg_ref[0].astype(f32), agg_ref[1].astype(f32)
+
+    def one_box(b):
+        rows_e, rows_x = [], []
         for i in range(per_box):
             p = perm_ref[b * per_box + i]
-            rows = slice(i * n_units, (i + 1) * n_units)
-            x_ref[rows, :] = cur_ref[p]
+            rows_x.append(cur_ref[p])
             c = cos_ref[pl.ds(p, 1), :]
             s = sin_ref[pl.ds(p, 1), :]
-            e_ref[rows, 0:n_dirs] = (c * agg_re - s * agg_im).astype(bf16)
-            e_ref[rows, n_dirs : 2 * n_dirs] = (s * agg_re + c * agg_im).astype(bf16)
+            rows_e.append(
+                jnp.concatenate([c * agg_re - s * agg_im, s * agg_re + c * agg_im], axis=1).astype(bf16)
+            )
         values = lax.dot_general(
-            e_ref[...], x_ref[...], (((0,), (0,)), ((), ())), preferred_element_type=f32
+            jnp.concatenate(rows_e, axis=0),
+            jnp.concatenate(rows_x, axis=0),
+            (((0,), (0,)), ((), ())),
+            preferred_element_type=f32,
         ).astype(bf16)
         for c in range(2):
             for q in range(n_sub):
                 at = c * n_dirs + q * quarter
                 box_ref[q, b, c] = values[at : at + quarter]
-        return carry
-
-    lax.fori_loop(0, n_box, one_box, 0)
-
-
-def near_part(located_ref, nb_ref, pad_ref, near_ref, a_ref, x_ref):
-    n_patch, n_slots, _ = nb_ref.shape
+
+    def two_boxes(h, carry):
+        one_box(2 * h)
+        one_box(2 * h + 1)
+        return carry
+
+    lax.fori_loop(0, n_box // 2, two_boxes, 0)
+
+
+def near_part(first, last, located_ref, nb_ref, pad_ref, near_ref, a_ref):
+    _, n_slots, rows_y, _ = nb_ref.shape
     n_units, n_sides = near_ref.shape[1:]
     lanes = lax.broadcasted_iota(jnp.int32, (8, 128), 1) // 32
 
@@ -56,12 +67,10 @@
             out = jnp.where(lanes == i, parts[i], out)
         return out
 
-    def one_patch(p, carry):
-        for q in range(8):
-            a_ref[q * 16 : q * 16 + n_slots, :] = nb_ref[p, :, q * 128 : (q + 1) * 128].astype(f32)
-        for j in range(n_slots):
-            x_ref[j * n_units : (j + 1) * n_units, :] = pad_ref[located_ref[p * n_slots + j]]
-        flat = [a_ref[pl.ds(j, 8, stride=16), :] for j in range(n_slots)]
+    def one_patch(x, y):
+        p = x * rows_y + y
+        found = [pad_ref[located_ref[j, x, y]] for j in range(n_slots)]
+        flat = [a_ref[pl.ds(j * 8 * rows_y + y, 8, stride=rows_y), :] for j in range(n_slots)]
         lhs = []
         for g in range(2):
             group = flat[g * 4 : g * 4 + 4]
@@ -72,70 +81,89 @@
             lhs.append(
                 jnp.concatenate([pick([rolled[(j - u) % 4] for j in range(4)]) for u in range(4)], axis=0)
             )
-        last = jnp.concatenate(
+        tail = jnp.concatenate(
             [flat[8]] + [pltpu.roll(flat[8], 128 - 32 * u, 1) for u in range(1, 4)], axis=0
         )
         total = jnp.dot(
-            jnp.concatenate(lhs, axis=1).astype(bf16), x_ref[0:256, :], preferred_element_type=f32
-        )
-        total += jnp.dot(
-            last[:, 0:n_units].astype(bf16), x_ref[256 : 256 + n_units, :], preferred_element_type=f32
-        )
+            jnp.concatenate(lhs, axis=1).astype(bf16),
+            jnp.concatenate(found[0:8], axis=0),
+            preferred_element_type=f32,
+        )
+        total += jnp.dot(tail[:, 0:n_units].astype(bf16), found[8], preferred_element_type=f32)
         for u in range(4):
             near_ref[p, pl.ds(u, 8, stride=4), :] = total[u * 8 : u * 8 + 8]
-        return carry
-
-    lax.fori_loop(0, n_patch, one_patch, 0)
-
-
-def far_part(perm_ref, slot_ref, lf_ref, dis_ref, cos_ref, sin_ref, near_ref, out_ref, d_ref, far_ref):
+
+    def one_row(x, carry):
+        for j in range(n_slots):
+            for q in range(8):
+                at = (j * 8 + q) * rows_y
+                a_ref[at : at + rows_y, :] = nb_ref[x, j, :, q * 128 : (q + 1) * 128].astype(f32)
+
+        def some(g, inner):
+            for i in range(4):
+                one_patch(x, g * 4 + i)
+            return inner
+
+        return lax.fori_loop(0, rows_y // 4, some, carry)
+
+    lax.fori_loop(first, last, one_row, 0)
+
+
+def far_part(perm_ref, slot_ref, lf_ref, dis_ref, cos_ref, sin_ref, near_ref, out_ref, far_ref):
     n_sub, n_box, _, quarter, n_sides = lf_ref.shape
     n_patch, n_dirs = cos_ref.shape
     n_units = near_ref.shape[1]
     per_box = n_patch // n_box
 
-    def one_box(b, carry):
-        dis_re, dis_im = dis_ref[0], dis_ref[1]
+    dis_re, dis_im = dis_ref[0].astype(f32), dis_ref[1].astype(f32)
+
+    def one_box(b):
+        rows_d = []
         for i in range(per_box):
             p = perm_ref[b * per_box + i]
-            rows = slice(i * n_units, (i + 1) * n_units)
             c = cos_ref[pl.ds(p, 1), :]
             s = sin_ref[pl.ds(p, 1), :]
-            d_ref[rows, 0:n_dirs] = (c * dis_re - s * dis_im).astype(bf16)
-            d_ref[rows, n_dirs : 2 * n_dirs] = (s * dis_re + c * dis_im).astype(bf16)
+            rows_d.append(
+                jnp.concatenate([c * dis_re - s * dis_im, s * dis_re + c * dis_im], axis=1).astype(bf16)
+            )
         field = jnp.concatenate([lf_ref[q, b, c] for c in range(2) for q in range(n_sub)], axis=0)
-        far = jnp.dot(d_ref[...], field, preferred_element_type=f32)
+        far = jnp.dot(jnp.concatenate(rows_d, axis=0), field, preferred_element_type=f32)
         for i in range(per_box):
             far_ref[b * per_box + i] = far[i * n_units : (i + 1) * n_units]
-        return carry
-
-    lax.fori_loop(0, n_box, one_box, 0)
-
-    def one_patch(p, carry):
-        out_ref[p] = (near_ref[p] + far_ref[slot_ref[p]]).astype(bf16)
-        return carry
-
-    lax.fori_loop(0, n_patch, one_patch, 0)
+
+    def two_boxes(h, carry):
+        one_box(2 * h)
+        one_box(2 * h + 1)
+        return carry
+
+    lax.fori_loop(0, n_box // 2, two_boxes, 0)
+
+    def some_patches(h, carry):
+        for i in range(8):
+            p = h * 8 + i
+            out_ref[p] = (near_ref[p] + far_ref[slot_ref[p]]).astype(bf16)
+        return carry
+
+    lax.fori_loop(0, n_patch // 8, some_patches, 0)
 
 
 def fused(
     n_strip, n_sub,
-    perm_ref, slot_ref, located_ref, cur_ref, nb_ref, angle_ref, agg_ref, dis_ref, centre_ref, shift_ref,
+    perm_ref, slot_ref, index_ref, cur_ref, nb_ref, angle_ref, agg_ref, dis_ref, centre_ref, shift_ref,
     out_ref,
-    pad_ref, box_ref, cos_ref, sin_ref, x_ref, e_ref, near_ref, a_ref, far_ref, lf_ref,
-    cen_ref, shf_ref, in_ref, wide_ref, w_ref, inc_ref, exp_ref, coef_ref, send_ref,
+    pad_ref, box_ref, cos_ref, sin_ref, near_ref, a_ref, far_ref, lf_ref,
+    cen_ref, shf_ref, in_ref, wide_ref, w_ref, inc_ref, exp_ref, coef_ref, send_ref, place_ref, located_ref, place_sem,
     halo_send, halo_recv, cen_send, cen_recv, shf_send, shf_recv, a2a_send, a2a_recv,
     exp_send, exp_recv, back_send, back_recv,
 ):
     strip = lax.axis_index("strip")
     sub = lax.axis_index("sub")
-    rows_x, rows_y = 4, 16
     rows_x, rows_y = cur_ref.shape[0], cur_ref.shape[1]
     n_units, n_sides = cur_ref.shape[2], cur_ref.shape[3]
     n_patch = rows_x * rows_y
     n_dirs = angle_ref.shape[1]
     quarter = n_dirs // n_sub
-    n_box = centre_ref.shape[0]
+    n_box = centre_ref.shape[1]
     all_box = n_box * n_sub
     wide_y = rows_y + 2
 
@@ -162,8 +190,17 @@
 
     lax.fori_loop(1, n_strip, greet, 0)
 
-    cen_ref[sub] = jnp.zeros((n_box, 128), f32)
-    cen_ref[sub, :, 0:2] = centre_ref[...]
+    cen_ref[sub] = jnp.zeros((8, 128), f32)
+    cen_ref[sub, 0:2, 0:n_box] = centre_ref[...]
+    wanted = index_ref[...]
+    ny_total = rows_y * n_sub
+    row = wanted // ny_total
+    place = (row - strip * rows_x + 1) * wide_y + (wanted - row * ny_total - sub * rows_y + 1)
+    empty = (rows_x + 2) * wide_y
+    place = jnp.minimum(jnp.maximum(place, 0), empty)
+    place_ref[...] = jnp.where(wanted >= 0, place, empty)
+    placing = pltpu.make_async_copy(place_ref, located_ref, place_sem)
+    placing.start()
     shf_ref[strip] = jnp.zeros((8, n_dirs), f32)
     shf_ref[strip, 0:2, :] = shift_ref[0]
     pl.semaphore_wait(barrier, 4 + n_sub - 1 + n_strip - 1)
@@ -216,7 +253,7 @@
     flat_cur = cur_ref.reshape(n_patch, n_units, n_sides)
     flat_pad = pad_ref.reshape((rows_x + 3) * wide_y, n_units, n_sides)
 
-    gather_boxes(perm_ref, flat_cur, angle_ref, agg_ref, box_ref, cos_ref, sin_ref, x_ref.at[0:256], e_ref)
+    gather_boxes(perm_ref, flat_cur, angle_ref, agg_ref, box_ref, cos_ref, sin_ref)
 
     def a2a_copy(d):
         return pltpu.make_async_remote_copy(
@@ -261,8 +298,8 @@
     coef_ref[...] = stacked.T
     here = coef_ref[pl.ds(pl.multiple_of(sub * quarter, quarter), quarter), :]
 
-    cen_col = cen_ref[...].reshape(all_box, 128)
-    cen_row = cen_col.T
+    cen_row = jnp.concatenate([cen_ref[i, :, 0:n_box] for i in range(n_sub)], axis=1)
+    cen_col = jnp.concatenate([cen_ref[i].T[0:n_box, :] for i in range(n_sub)], axis=0)
     col_x, col_y = cen_col[:, 0:1], cen_col[:, 1:2]
     row_x, row_y = cen_row[0:1, :], cen_row[1:2, :]
     step = 2.0 * math.pi / n_dirs
@@ -297,6 +334,13 @@
 
     lax.fori_loop(0, quarter // fold, weights, 0)
 
+    placing.wait()
+    for n in range(len(offsets)):
+        halo_copy(n).wait_recv()
+    split = NSPLIT * rows_x // 4
+    later = LATER * rows_x // 4
+    near_part(0, split, located_ref, nb_ref, flat_pad, near_ref, a_ref)
+
     def source(d):
         return lax.rem(sub + n_sub - d, n_sub)
 
@@ -327,20 +371,22 @@
 
     lax.fori_loop(1, n_strip, send_exp, 0)
 
-    def interact(k, carry):
-        rhs = wide_ref[pl.ds(k, 2 * all_box, stride=quarter), :].astype(bf16)
-        inc_ref[pl.ds(k, 2 * all_box, stride=quarter), :] = jnp.dot(
-            w_ref[k], rhs, preferred_element_type=f32
-        )
-        return carry
-
-    lax.fori_loop(0, quarter, interact, 0)
+    def interact(g, carry):
+        ks = [g * 8 + i for i in range(8)]
+        rhs = [wide_ref[pl.ds(k, 2 * all_box, stride=quarter), :].astype(bf16) for k in ks]
+        out = [jnp.dot(w_ref[k], v, preferred_element_type=f32) for k, v in zip(ks, rhs)]
+        for k, v in zip(ks, out):
+            inc_ref[pl.ds(k, 2 * all_box, stride=quarter), :] = v
+        return carry
+
+    lax.fori_loop(0, quarter // 8, interact, 0)
 
     def wait_exp(d, carry):
         src = lax.rem(strip + n_strip - d, n_strip)
         strip_copy(exp_ref, exp_send, exp_recv, d, src).wait_recv()
         return carry
 
+    near_part(split, later, located_ref, nb_ref, flat_pad, near_ref, a_ref)
     lax.fori_loop(1, n_strip, wait_exp, 0)
     field_re = jnp.zeros((quarter, n_sides), f32)
     field_im = jnp.zeros((quarter, n_sides), f32)
@@ -349,36 +395,39 @@
         v_re, v_im = exp_ref[q, 0].astype(f32), exp_ref[q, 1].astype(f32)
         field_re += c_re * v_re - c_im * v_im
         field_im += c_re * v_im + c_im * v_re
+    def back_copy(d, at, to):
+        return pltpu.make_async_remote_copy(
+            src_ref=send_ref.at[to], dst_ref=lf_ref.at[at],
+            send_sem=back_send.at[d], recv_sem=back_recv.at[d],
+            device_id=(strip, to), device_id_type=MESH,
+        )
+
     for b in range(all_box):
         p_re, p_im = psi_re[:, b : b + 1], psi_im[:, b : b + 1]
         v_re = inc_ref[b * quarter : (b + 1) * quarter, :]
         v_im = inc_ref[(all_box + b) * quarter : (all_box + b + 1) * quarter, :]
         send_ref[b // n_box, b % n_box, 0] = (v_re + p_re * field_re + p_im * field_im).astype(bf16)
         send_ref[b // n_box, b % n_box, 1] = (v_im + p_re * field_im - p_im * field_re).astype(bf16)
-
-    def back_copy(d, at):
-        return pltpu.make_async_remote_copy(
-            src_ref=send_ref.at[sub_peer(d)], dst_ref=lf_ref.at[at],
-            send_sem=back_send.at[d], recv_sem=back_recv.at[d],
-            device_id=(strip, sub_peer(d)), device_id_type=MESH,
-        )
+        if b % n_box == n_box - 1:
+            to = b // n_box
+
+            @pl.when(to != sub)
+            def _(to=to):
+                back_copy(lax.rem(to - sub + n_sub, n_sub), sub, to).start()
+
+
+    lf_ref[sub] = send_ref[sub]
+
+    near_part(later, rows_x, located_ref, nb_ref, flat_pad, near_ref, a_ref)
 
     for d in range(1, n_sub):
-        back_copy(d, sub).start()
-    lf_ref[sub] = send_ref[sub]
-
-    for n in range(len(offsets)):
-        halo_copy(n).wait_recv()
-    near_part(located_ref, nb_ref, flat_pad, near_ref, a_ref, x_ref)
-
-    for d in range(1, n_sub):
-        back_copy(d, source(d)).wait_recv()
-    far_part(perm_ref, slot_ref, lf_ref, dis_ref, cos_ref, sin_ref, near_ref, out_ref, e_ref, far_ref)
+        back_copy(d, source(d), sub_peer(d)).wait_recv()
+    far_part(perm_ref, slot_ref, lf_ref, dis_ref, cos_ref, sin_ref, near_ref, out_ref, far_ref)
 
     for d in range(1, n_sub):
         cen_copy(d).wait_send()
         a2a_copy(d).wait_send()
-        back_copy(d, sub).wait_send()
+        back_copy(d, sub, sub_peer(d)).wait_send()
 
     def drain(d, carry):
         strip_copy(shf_ref, shf_send, shf_recv, d, strip).wait_send()
@@ -408,16 +457,8 @@
     box_dev = box_centre.shape[0]
     n_sub = lax.axis_size("sub")
     n_strip = lax.axis_size("strip")
-    strip_pos = lax.axis_index("strip")
-    sub_pos = lax.axis_index("sub")
-    ny_total = rows_y * n_sub
     quarter = n_dirs // n_sub
     all_box = box_dev * n_sub
-    wanted = near_index.reshape(n_patch * n_slots)
-    located = (wanted // ny_total - strip_pos * rows_x + 1) * (rows_y + 2) + (
-        wanted % ny_total - sub_pos * rows_y + 1
-    )
-    located = jnp.where(wanted >= 0, located, (rows_x + 2) * (rows_y + 2))
     ids = jnp.arange(n_patch, dtype=jnp.int32)
     key = box_of_patch.reshape(n_patch) * n_patch + ids
     slot = jnp.sum((key[None, :] < key[:, None]).astype(jnp.int32), axis=1)
@@ -430,13 +471,11 @@
         pltpu.VMEM((n_sub, box_dev, 2, quarter, n_sides), bf16),
         pltpu.VMEM((n_patch, n_dirs), f32),
         pltpu.VMEM((n_patch, n_dirs), f32),
-        pltpu.VMEM((n_slots * n_units, n_sides), bf16),
-        pltpu.VMEM((n_patch // box_dev * n_units, 2 * n_dirs), bf16),
         pltpu.VMEM((n_patch, n_units, n_sides), f32),
-        pltpu.VMEM((128, 128), f32),
+        pltpu.VMEM((n_slots * 8 * rows_y, 128), f32),
         pltpu.VMEM((n_patch, n_units, n_sides), f32),
         pltpu.VMEM((n_sub, box_dev, 2, quarter, n_sides), bf16),
-        pltpu.VMEM((n_sub, box_dev, 128), f32),
+        pltpu.VMEM((n_sub, 8, 128), f32),
         pltpu.VMEM((n_strip, 8, n_dirs), f32),
         pltpu.VMEM((n_sub, box_dev, 2, quarter, n_sides), bf16),
         pltpu.VMEM((2 * all_box * quarter, n_sides), f32),
@@ -445,6 +484,9 @@
         pltpu.VMEM((n_strip, 2, quarter, n_sides), bf16),
         pltpu.VMEM((n_dirs, 2 * n_strip), f32),
         pltpu.VMEM((n_sub, box_dev, 2, quarter, n_sides), bf16),
+        pltpu.VMEM((n_slots, rows_x, rows_y), jnp.int32),
+        pltpu.SMEM((n_slots, rows_x, rows_y), jnp.int32),
+        dma(()),
         dma((8,)), dma((8,)),
         dma((n_sub,)), dma((n_sub,)),
         dma((n_strip,)), dma((n_strip,)),
@@ -455,7 +497,7 @@
     result = pl.pallas_call(
         functools.partial(fused, n_strip, n_sub),
         out_shape=jax.ShapeDtypeStruct((n_patch, n_units, n_sides), bf16),
-        in_specs=[smem] * 3 + [vmem] * 7,
+        in_specs=[smem] * 2 + [vmem] * 8,
         out_specs=vmem,
         scratch_shapes=scratch,
         compiler_params=pltpu.CompilerParams(
@@ -464,13 +506,13 @@
     )(
         perm,
         slot,
-        located,
+        jnp.transpose(near_index, (2, 0, 1)),
         currents,
-        near_blocks.reshape(n_patch, n_slots, n_units * n_units),
+        jnp.transpose(near_blocks, (0, 2, 1, 3)),
         patch_angle.reshape(n_patch, n_dirs),
-        jnp.swapaxes(aggregation, 1, 2).astype(f32),
-        jnp.swapaxes(disaggregation, 1, 2).astype(f32),
-        box_centre,
+        jnp.swapaxes(aggregation, 1, 2),
+        jnp.swapaxes(disaggregation, 1, 2),
+        box_centre.T,
         strip_shift,
     )
     return result.reshape(rows_x, rows_y, n_units, n_sides)

time: 47 us -> 37.2 us (0.79)
  Pallas kernels: 40.1 us -> 28.1 us
  local copies, waits for them, and re-layouts: 4.64 us -> 7.46 us
  other arithmetic: 1.8 us -> 0.98 us
    pallas_call x1, Pallas kernels: 40.1 us -> 28.1 us  [per_device(): pl.pallas_call(functools.partial(fused, n_strip, n_sub), out_shape=jax.Sh...]
    unnamed x10 -> x17, local copies, waits for them, and re-layouts: 4.42 us -> 7.38 us
    convert_element_type x1 -> x0, other arithmetic: 0.74 us -> none  [per_device(): jnp.swapaxes(disaggregation, 1, 2).astype(f32)]
where the time goes in v1:
time: 37.2 us; the launch traced here: 36.6 us
  Pallas kernels  28.1 us (76%)
  local copies, waits for them, and re-layouts  7.46 us (20%)
  other arithmetic  0.98 us (3%)
    pallas_call x1, Pallas kernels, per_device(): pl.pallas_call(functools.partial(fused, n_strip, n_sub), out_shape=jax.Sh...  28.1 us
    unnamed x17, local copies, waits for them, and re-layouts  7.38 us

profile of v1, /device:TPU:1, one launch (start us, length us, event | category | flops | bytes accessed | tf_op | source)
XLA Modules:
  0.0 36.6 jit_solution(17573867247391832104)
XLA Ops:
  0.0 0.7 %broadcast_multiply_fusion = s32[4,16]{1,0:T(4,128)S(1)} fusion(s32[4,16]{1,0:T(4,128)} %param.12), kind=kLoop, calls=%fused_computation.3 | loop fusion | flops 64 | bytes 512 | tf_op jit(solution)/shard_map/mul | solution.py:463
  0.7 0.1 mul.19
  0.8 0.2 convert_reduce_fusion.slot_ref
  1.0 0.1 select_reduce_fusion.perm_ref
  1.1 0.0 copy-start
  1.1 1.3 %copy-done = bf16[4,16,9,1024]{3,1,2,0:T(8,128)(2,1)S(1)} copy-done((bf16[4,16,9,1024]{3,1,2,0:T(8,128)(2,1)S(1)}, bf16[4,16,9,1024]{3,1,2,0:T(8,128)(2,1)}, u32[]{:S(2)}) %copy-start) | copy-done | bytes 1179672
  2.4 0.0 copy-start.1
  2.4 1.0 %copy-done.1 = bf16[4,16,32,128]{3,2,1,0:T(8,128)(2,1)S(1)} copy-done((bf16[4,16,32,128]{3,2,1,0:T(8,128)(2,1)S(1)}, bf16[4,16,32,128]{3,2,1,0:T(8,128)(2,1)}, u32[]{:S(2)}) %copy-start.1) | copy-done | bytes 524312
  3.4 0.0 copy-start.2
  3.4 0.8 %copy-done.2 = f32[4,16,128]{2,1,0:T(8,128)S(1)} copy-done((f32[4,16,128]{2,1,0:T(8,128)S(1)}, f32[4,16,128]{2,1,0:T(8,128)}, u32[]{:S(2)}) %copy-start.2) | copy-done | bytes 32792
  4.2 0.0 copy-start.3
  4.2 0.7 %copy-done.3 = s32[4,16,9]{1,0,2:T(4,128)S(1)} copy-done((s32[4,16,9]{1,0,2:T(4,128)S(1)}, s32[4,16,9]{1,0,2:T(4,128)}, u32[]{:S(2)}) %copy-start.3) | copy-done | bytes 2328
  4.9 0.0 copy-start.4
  4.9 0.7 %copy-done.4 = bf16[2,128,32]{1,2,0:T(8,128)(2,1)S(1)} copy-done((bf16[2,128,32]{1,2,0:T(8,128)(2,1)S(1)}, bf16[2,128,32]{1,2,0:T(8,128)(2,1)}, u32[]{:S(2)}) %copy-start.4) | copy-done | bytes 16408
  5.6 0.0 copy-start.5
  5.6 0.7 %copy-done.5 = bf16[2,128,32]{1,2,0:T(8,128)(2,1)S(1)} copy-done((bf16[2,128,32]{1,2,0:T(8,128)(2,1)S(1)}, bf16[2,128,32]{1,2,0:T(8,128)(2,1)}, u32[]{:S(2)}) %copy-start.5) | copy-done | bytes 16408
  6.3 0.0 copy-start.6
  6.3 0.7 %copy-done.6 = f32[8,2]{0,1:T(2,128)S(1)} copy-done((f32[8,2]{0,1:T(2,128)S(1)}, f32[8,2]{0,1:T(2,128)}, u32[]{:S(2)}) %copy-start.6) | copy-done | bytes 88
  7.0 0.0 copy-start.7
  7.0 0.7 %copy-done.7 = f32[1,2,128]{2,1,0:T(2,128)S(1)} copy-done((f32[1,2,128]{2,1,0:T(2,128)S(1)}, f32[1,2,128]{2,1,0:T(2,128)}, u32[]{:S(2)}) %copy-start.7) | copy-done | bytes 1048
  7.7 28.1 %shard_map.91 = bf16[64,32,128]{2,1,0:T(8,128)(2,1)S(1)} custom-call(s32[64]{0:T(128)S(1)} %select_reduce_fusion.perm_ref, s32[64]{0:T(128)S(1)} %convert_reduce_fusion.slot_ref, s32[9,4,16]{2,1,0:T(4,128)S(1)} %bitcast.10, bf16[4,16,32,128]{3,2,1,0:T(8,128)(2,1)S(1)} %copy-done.1, bf16[4,9,16,1024]{3,2,1,0:T(8,128)(2,1)S(1)} %bitcast.8, ...), custom_call_target="tpu_custom_call" | custom-call | tf_op jit(solution)/shard_map/pallas_call | solution.py:497
  35.8 0.8 %copy.11 = bf16[4,16,32,128]{3,2,1,0:T(8,128)(2,1)} copy(bf16[4,16,32,128]{3,2,1,0:T(8,128)(2,1)S(1)} %bitcast.7) | data formatting | bytes 1048576
  (1 shorter events, 0.0 us)
Async XLA Ops:
  1.1 1.3 %copy-start = (bf16[4,16,9,1024]{3,1,2,0:T(8,128)(2,1)S(1)}, bf16[4,16,9,1024]{3,1,2,0:T(8,128)(2,1)}, u32[]{:S(2)}) copy-start(bf16[4,16,9,1024]{3,1,2,0:T(8,128)(2,1)} %param.10) | copy-start | bytes 3538948
  2.4 1.0 %copy-start.1 = (bf16[4,16,32,128]{3,2,1,0:T(8,128)(2,1)S(1)}, bf16[4,16,32,128]{3,2,1,0:T(8,128)(2,1)}, u32[]{:S(2)}) copy-start(bf16[4,16,32,128]{3,2,1,0:T(8,128)(2,1)} %cur_ref.1) | copy-start | bytes 1572868
  3.4 0.8 %copy-start.2 = (f32[4,16,128]{2,1,0:T(8,128)S(1)}, f32[4,16,128]{2,1,0:T(8,128)}, u32[]{:S(2)}) copy-start(f32[4,16,128]{2,1,0:T(8,128)} %param.14) | copy-start | bytes 98308
  4.2 0.7 %copy-start.3 = (s32[4,16,9]{1,0,2:T(4,128)S(1)}, s32[4,16,9]{1,0,2:T(4,128)}, u32[]{:S(2)}) copy-start(s32[4,16,9]{1,0,2:T(4,128)} %param.11) | copy-start | bytes 6916
  4.9 0.7 %copy-start.4 = (bf16[2,128,32]{1,2,0:T(8,128)(2,1)S(1)}, bf16[2,128,32]{1,2,0:T(8,128)(2,1)}, u32[]{:S(2)}) copy-start(bf16[2,128,32]{1,2,0:T(8,128)(2,1)} %param.15) | copy-start | bytes 49156
  5.6 0.7 %copy-start.5 = (bf16[2,128,32]{1,2,0:T(8,128)(2,1)S(1)}, bf16[2,128,32]{1,2,0:T(8,128)(2,1)}, u32[]{:S(2)}) copy-start(bf16[2,128,32]{1,2,0:T(8,128)(2,1)} %param.16) | copy-start | bytes 49156
  6.3 0.7 %copy-start.6 = (f32[8,2]{0,1:T(2,128)S(1)}, f32[8,2]{0,1:T(2,128)}, u32[]{:S(2)}) copy-start(f32[8,2]{0,1:T(2,128)} %param.13) | copy-start | bytes 196
  7.0 0.7 %copy-start.7 = (f32[1,2,128]{2,1,0:T(2,128)S(1)}, f32[1,2,128]{2,1,0:T(2,128)}, u32[]{:S(2)}) copy-start(f32[1,2,128]{2,1,0:T(2,128)} %shift_ref.1) | copy-start | bytes 3076

commit v2 on v1

--- a/solution.py
+++ b/solution.py
@@ -149,8 +149,9 @@
 
 def fused(
     n_strip, n_sub,
-    perm_ref, slot_ref, index_ref, cur_ref, nb_ref, angle_ref, agg_ref, dis_ref, centre_ref, shift_ref,
+    perm_ref, slot_ref, index_in, cur_in, nb_in, angle_in, agg_in, dis_in, centre_in, shift_in,
     out_ref,
+    index_ref, cur_ref, nb_ref, angle_ref, agg_ref, dis_ref, centre_ref, shift_ref, load_sem,
     pad_ref, box_ref, cos_ref, sin_ref, near_ref, a_ref, far_ref, lf_ref,
     cen_ref, shf_ref, in_ref, wide_ref, w_ref, inc_ref, exp_ref, coef_ref, send_ref, place_ref, located_ref, place_sem,
     halo_send, halo_recv, cen_send, cen_recv, shf_send, shf_recv, a2a_send, a2a_recv,
@@ -175,6 +176,14 @@
 
     offsets = [(dx, dy) for dx in (-1, 0, 1) for dy in (-1, 0, 1) if dx or dy]
 
+    pairs = [
+        (index_in, index_ref), (centre_in, centre_ref), (shift_in, shift_ref), (cur_in, cur_ref),
+        (angle_in, angle_ref), (agg_in, agg_ref), (nb_in, nb_ref), (dis_in, dis_ref),
+    ]
+    loads = [pltpu.make_async_copy(a, b, load_sem.at[i]) for i, (a, b) in enumerate(pairs)]
+    for load in loads:
+        load.start()
+
     barrier = pltpu.get_barrier_semaphore()
     for dx in (-1, 1):
         for dy in (-1, 1):
@@ -190,6 +199,8 @@
 
     lax.fori_loop(1, n_strip, greet, 0)
 
+    for load in loads[0:3]:
+        load.wait()
     cen_ref[sub] = jnp.zeros((8, 128), f32)
     cen_ref[sub, 0:2, 0:n_box] = centre_ref[...]
     wanted = index_ref[...]
@@ -239,6 +250,7 @@
             device_id=(strip_peer(dx + n_strip), sub_peer(dy + n_sub)), device_id_type=MESH,
         )
 
+    loads[3].wait()
     for d in range(1, n_sub):
         cen_copy(d).start()
 
@@ -250,6 +262,8 @@
     for n in range(len(offsets)):
         halo_copy(n).start()
 
+    loads[4].wait()
+    loads[5].wait()
     flat_cur = cur_ref.reshape(n_patch, n_units, n_sides)
     flat_pad = pad_ref.reshape((rows_x + 3) * wide_y, n_units, n_sides)
 
@@ -335,6 +349,8 @@
     lax.fori_loop(0, quarter // fold, weights, 0)
 
     placing.wait()
+    loads[6].wait()
+    loads[7].wait()
     for n in range(len(offsets)):
         halo_copy(n).wait_recv()
     split = NSPLIT * rows_x // 4
@@ -466,7 +482,19 @@
     smem = pl.BlockSpec(memory_space=pltpu.SMEM)
     vmem = pl.BlockSpec(memory_space=pltpu.VMEM)
     dma = pltpu.SemaphoreType.DMA
-    scratch = [
+    operands = (
+        jnp.transpose(near_index, (2, 0, 1)),
+        currents,
+        jnp.transpose(near_blocks, (0, 2, 1, 3)),
+        patch_angle.reshape(n_patch, n_dirs),
+        jnp.swapaxes(aggregation, 1, 2),
+        jnp.swapaxes(disaggregation, 1, 2),
+        box_centre.T,
+        strip_shift,
+    )
+    hbm = pl.BlockSpec(memory_space=pltpu.HBM)
+    scratch = [pltpu.VMEM(a.shape, a.dtype) for a in operands] + [
+        dma((8,)),
         pltpu.VMEM((rows_x + 3, rows_y + 2, n_units, n_sides), bf16),
         pltpu.VMEM((n_sub, box_dev, 2, quarter, n_sides), bf16),
         pltpu.VMEM((n_patch, n_dirs), f32),
@@ -497,23 +525,16 @@
     result = pl.pallas_call(
         functools.partial(fused, n_strip, n_sub),
         out_shape=jax.ShapeDtypeStruct((n_patch, n_units, n_sides), bf16),
-        in_specs=[smem] * 2 + [vmem] * 8,
+        in_specs=[smem] * 2 + [hbm] * 8,
         out_specs=vmem,
         scratch_shapes=scratch,
         compiler_params=pltpu.CompilerParams(
-            collective_id=0, has_side_effects=True, vmem_limit_bytes=48 * 1024 * 1024
+            collective_id=0, has_side_effects=True, vmem_limit_bytes=60 * 1024 * 1024
         ),
     )(
         perm,
         slot,
-        jnp.transpose(near_index, (2, 0, 1)),
-        currents,
-        jnp.transpose(near_blocks, (0, 2, 1, 3)),
-        patch_angle.reshape(n_patch, n_dirs),
-        jnp.swapaxes(aggregation, 1, 2),
-        jnp.swapaxes(disaggregation, 1, 2),
-        box_centre.T,
-        strip_shift,
+        *operands,
     )
     return result.reshape(rows_x, rows_y, n_units, n_sides)
 

time: 37.2 us -> 32.8 us (0.88)
  local copies, waits for them, and re-layouts: 7.46 us -> 1.96 us
  Pallas kernels: 28.1 us -> 29.1 us
  other arithmetic: 0.98 us -> 1.49 us
    unnamed x17 -> x3, local copies, waits for them, and re-layouts: 7.38 us -> 1.87 us
    pallas_call x1, Pallas kernels: 28.1 us -> 29.1 us  [per_device(): pl.pallas_call(functools.partial(fused, n_strip, n_sub), out_shape=jax.Sh...]
    reduce_sum x1, other arithmetic: 0.12 us -> 0.63 us  [per_device(): jnp.sum(jnp.where(slot[None, :] == ids[:, None], ids[None, :], 0), axis=1)]
where the time goes in v2:
time: 32.8 us; the launch traced here: 32.6 us
  Pallas kernels  29.1 us (89%)
  local copies, waits for them, and re-layouts  1.96 us (6%)
  other arithmetic  1.49 us (5%)
    pallas_call x1, Pallas kernels, per_device(): pl.pallas_call(functools.partial(fused, n_strip, n_sub), out_shape=jax.Sh...  29.1 us
    unnamed x3, local copies, waits for them, and re-layouts  1.87 us
    mul x1, other arithmetic, per_device(): key = box_of_patch.reshape(n_patch) * n_patch + ids  0.68 us

profile of v2, /device:TPU:1, one launch (start us, length us, event | category | flops | bytes accessed | tf_op | source)
XLA Modules:
  0.0 32.6 jit_solution(14829459782289174123)
XLA Ops:
  0.0 0.7 %broadcast_multiply_fusion = s32[4,16]{1,0:T(4,128)S(1)} fusion(s32[4,16]{1,0:T(4,128)} %param.12), kind=kLoop, calls=%fused_computation.3 | loop fusion | flops 64 | bytes 512 | tf_op jit(solution)/shard_map/mul | solution.py:479
  0.7 0.1 mul.19
  0.8 0.2 convert_reduce_fusion.slot_ref
  1.0 0.0 copy-start
  1.0 0.6 %select_reduce_fusion.perm_ref = s32[64]{0:T(128)} fusion(s32[64]{0:T(128)S(1)} %convert_reduce_fusion.slot_ref), kind=kLoop, calls=%fused_computation | loop fusion | flops 12224 | bytes 512 | tf_op jit(solution)/shard_map/reduce_sum | solution.py:481
  1.6 0.0 copy-done
  1.6 29.1 %shard_map.91 = bf16[64,32,128]{2,1,0:T(8,128)(2,1)} custom-call(s32[64]{0:T(128)} %select_reduce_fusion.perm_ref, s32[64]{0:T(128)} %copy-done, s32[9,4,16]{2,1,0:T(4,128)} %bitcast.10, bf16[4,16,32,128]{3,2,1,0:T(8,128)(2,1)} %cur_in.1, bf16[4,9,16,1024]{3,2,1,0:T(8,128)(2,1)} %bitcast.8, f32[64,128]{1,0:T(8,128)} %bitcast.9, ...), custom_call_target="tpu_custom_call" | custom-call | tf_op jit(solution)/shard_map/pallas_call | solution.py:525
  30.7 1.9 %copy.11 = bf16[4,16,32,128]{3,2,1,0:T(8,128)(2,1)} copy(bf16[4,16,32,128]{3,2,1,0:T(8,128)(2,1)} %bitcast.7) | data formatting | bytes 1048576
  (1 shorter events, 0.0 us)
Async XLA Ops:
  1.0 0.6 %copy-start = (s32[64]{0:T(128)}, s32[64]{0:T(128)S(1)}, u32[]{:S(2)}) copy-start(s32[64]{0:T(128)S(1)} %convert_reduce_fusion.slot_ref) | copy-start | bytes 772

commit v3 on v2

--- a/solution.py
+++ b/solution.py
@@ -10,8 +10,6 @@
 
 wave_number = 1.5
 strip_weight = 0.03
-NSPLIT = 1
-LATER = 2
 MESH = pl.DeviceIdType.MESH
 f32 = jnp.float32
 bf16 = jnp.bfloat16
@@ -259,8 +257,6 @@
         return carry
 
     lax.fori_loop(1, n_strip, send_shift, 0)
-    for n in range(len(offsets)):
-        halo_copy(n).start()
 
     loads[4].wait()
     loads[5].wait()
@@ -278,6 +274,8 @@
 
     for d in range(1, n_sub):
         a2a_copy(d).start()
+    for n in range(len(offsets)):
+        halo_copy(n).start()
 
     for x in range(rows_x):
         pad_ref[x + 1, 1 : rows_y + 1] = cur_ref[x]
@@ -351,11 +349,6 @@
     placing.wait()
     loads[6].wait()
     loads[7].wait()
-    for n in range(len(offsets)):
-        halo_copy(n).wait_recv()
-    split = NSPLIT * rows_x // 4
-    later = LATER * rows_x // 4
-    near_part(0, split, located_ref, nb_ref, flat_pad, near_ref, a_ref)
 
     def source(d):
         return lax.rem(sub + n_sub - d, n_sub)
@@ -402,7 +395,6 @@
         strip_copy(exp_ref, exp_send, exp_recv, d, src).wait_recv()
         return carry
 
-    near_part(split, later, located_ref, nb_ref, flat_pad, near_ref, a_ref)
     lax.fori_loop(1, n_strip, wait_exp, 0)
     field_re = jnp.zeros((quarter, n_sides), f32)
     field_im = jnp.zeros((quarter, n_sides), f32)
@@ -434,7 +426,9 @@
 
     lf_ref[sub] = send_ref[sub]
 
-    near_part(later, rows_x, located_ref, nb_ref, flat_pad, near_ref, a_ref)
+    for n in range(len(offsets)):
+        halo_copy(n).wait_recv()
+    near_part(0, rows_x, located_ref, nb_ref, flat_pad, near_ref, a_ref)
 
     for d in range(1, n_sub):
         back_copy(d, source(d), sub_peer(d)).wait_recv()

time: 32.8 us -> 32.1 us (0.979)
  Pallas kernels: 29.1 us -> 28.4 us
    pallas_call x1, Pallas kernels: 29.1 us -> 28.4 us  [per_device(): pl.pallas_call(functools.partial(fused, n_strip, n_sub), out_shape=jax.Sh...]
where the time goes in v3:
time: 32.1 us; the launch traced here: 31.9 us
  Pallas kernels  28.4 us (88%)
  local copies, waits for them, and re-layouts  1.96 us (6%)
  other arithmetic  1.49 us (5%)
    pallas_call x1, Pallas kernels, per_device(): pl.pallas_call(functools.partial(fused, n_strip, n_sub), out_shape=jax.Sh...  28.4 us
    unnamed x3, local copies, waits for them, and re-layouts  1.87 us
    mul x1, other arithmetic, per_device(): key = box_of_patch.reshape(n_patch) * n_patch + ids  0.68 us

profile of v3, /device:TPU:1, one launch (start us, length us, event | category | flops | bytes accessed | tf_op | source)
XLA Modules:
  0.0 31.9 jit_solution(15068988148045098085)
XLA Ops:
  0.0 0.7 %broadcast_multiply_fusion = s32[4,16]{1,0:T(4,128)S(1)} fusion(s32[4,16]{1,0:T(4,128)} %param.12), kind=kLoop, calls=%fused_computation.3 | loop fusion | flops 64 | bytes 512 | tf_op jit(solution)/shard_map/mul | solution.py:473
  0.7 0.1 mul.19
  0.8 0.2 convert_reduce_fusion.slot_ref
  1.0 0.0 copy-start
  1.0 0.6 %select_reduce_fusion.perm_ref = s32[64]{0:T(128)} fusion(s32[64]{0:T(128)S(1)} %convert_reduce_fusion.slot_ref), kind=kLoop, calls=%fused_computation | loop fusion | flops 12224 | bytes 512 | tf_op jit(solution)/shard_map/reduce_sum | solution.py:475
  1.6 0.0 copy-done
  1.6 28.4 %shard_map.91 = bf16[64,32,128]{2,1,0:T(8,128)(2,1)} custom-call(s32[64]{0:T(128)} %select_reduce_fusion.perm_ref, s32[64]{0:T(128)} %copy-done, s32[9,4,16]{2,1,0:T(4,128)} %bitcast.10, bf16[4,16,32,128]{3,2,1,0:T(8,128)(2,1)} %cur_in.1, bf16[4,9,16,1024]{3,2,1,0:T(8,128)(2,1)} %bitcast.8, f32[64,128]{1,0:T(8,128)} %bitcast.9, ...), custom_call_target="tpu_custom_call" | custom-call | tf_op jit(solution)/shard_map/pallas_call | solution.py:519
  30.0 1.9 %copy.11 = bf16[4,16,32,128]{3,2,1,0:T(8,128)(2,1)} copy(bf16[4,16,32,128]{3,2,1,0:T(8,128)(2,1)} %bitcast.7) | data formatting | bytes 1048576
  (1 shorter events, 0.0 us)
Async XLA Ops:
  1.0 0.6 %copy-start = (s32[64]{0:T(128)}, s32[64]{0:T(128)S(1)}, u32[]{:S(2)}) copy-start(s32[64]{0:T(128)S(1)} %convert_reduce_fusion.slot_ref) | copy-start | bytes 772

commit v4 on v3

--- a/solution.py
+++ b/solution.py
@@ -107,25 +107,33 @@
     lax.fori_loop(first, last, one_row, 0)
 
 
-def far_part(perm_ref, slot_ref, lf_ref, dis_ref, cos_ref, sin_ref, near_ref, out_ref, far_ref):
-    n_sub, n_box, _, quarter, n_sides = lf_ref.shape
-    n_patch, n_dirs = cos_ref.shape
-    n_units = near_ref.shape[1]
-    per_box = n_patch // n_box
-
+def far_matrices(perm_ref, dis_ref, cos_ref, sin_ref, d_ref):
+    n_box, rows, _ = d_ref.shape
+    n_units = dis_ref.shape[1]
+    per_box = rows // n_units
     dis_re, dis_im = dis_ref[0].astype(f32), dis_ref[1].astype(f32)
 
-    def one_box(b):
-        rows_d = []
+    def one_box(b, carry):
         for i in range(per_box):
             p = perm_ref[b * per_box + i]
             c = cos_ref[pl.ds(p, 1), :]
             s = sin_ref[pl.ds(p, 1), :]
-            rows_d.append(
-                jnp.concatenate([c * dis_re - s * dis_im, s * dis_re + c * dis_im], axis=1).astype(bf16)
-            )
+            d_ref[b, i * n_units : (i + 1) * n_units, :] = jnp.concatenate(
+                [c * dis_re - s * dis_im, s * dis_re + c * dis_im], axis=1
+            ).astype(bf16)
+        return carry
+
+    lax.fori_loop(0, n_box, one_box, 0)
+
+
+def far_part(slot_ref, lf_ref, d_ref, near_ref, out_ref, far_ref):
+    n_sub, n_box, _, quarter, n_sides = lf_ref.shape
+    n_patch, n_units, _ = near_ref.shape
+    per_box = n_patch // n_box
+
+    def one_box(b):
         field = jnp.concatenate([lf_ref[q, b, c] for c in range(2) for q in range(n_sub)], axis=0)
-        far = jnp.dot(jnp.concatenate(rows_d, axis=0), field, preferred_element_type=f32)
+        far = jnp.dot(d_ref[b], field, preferred_element_type=f32)
         for i in range(per_box):
             far_ref[b * per_box + i] = far[i * n_units : (i + 1) * n_units]
 
@@ -151,7 +159,7 @@
     out_ref,
     index_ref, cur_ref, nb_ref, angle_ref, agg_ref, dis_ref, centre_ref, shift_ref, load_sem,
     pad_ref, box_ref, cos_ref, sin_ref, near_ref, a_ref, far_ref, lf_ref,
-    cen_ref, shf_ref, in_ref, wide_ref, w_ref, inc_ref, exp_ref, coef_ref, send_ref, place_ref, located_ref, place_sem,
+    cen_ref, shf_ref, in_ref, wide_ref, w_ref, inc_ref, exp_ref, coef_ref, send_ref, d_ref, place_ref, located_ref, place_sem,
     halo_send, halo_recv, cen_send, cen_recv, shf_send, shf_recv, a2a_send, a2a_recv,
     exp_send, exp_recv, back_send, back_recv,
 ):
@@ -349,6 +357,7 @@
     placing.wait()
     loads[6].wait()
     loads[7].wait()
+    far_matrices(perm_ref, dis_ref, cos_ref, sin_ref, d_ref)
 
     def source(d):
         return lax.rem(sub + n_sub - d, n_sub)
@@ -432,7 +441,7 @@
 
     for d in range(1, n_sub):
         back_copy(d, source(d), sub_peer(d)).wait_recv()
-    far_part(perm_ref, slot_ref, lf_ref, dis_ref, cos_ref, sin_ref, near_ref, out_ref, far_ref)
+    far_part(slot_ref, lf_ref, d_ref, near_ref, out_ref, far_ref)
 
     for d in range(1, n_sub):
         cen_copy(d).wait_send()
@@ -506,6 +515,7 @@
         pltpu.VMEM((n_strip, 2, quarter, n_sides), bf16),
         pltpu.VMEM((n_dirs, 2 * n_strip), f32),
         pltpu.VMEM((n_sub, box_dev, 2, quarter, n_sides), bf16),
+        pltpu.VMEM((box_dev, n_patch // box_dev * n_units, 2 * n_dirs), bf16),
         pltpu.VMEM((n_slots, rows_x, rows_y), jnp.int32),
         pltpu.SMEM((n_slots, rows_x, rows_y), jnp.int32),
         dma(()),

time: 32.1 us -> 32.2 us (level)
  no operation moved by 1% of the time
where the time goes in v4:
time: 32.2 us; the launch traced here: 32 us
  Pallas kernels  28.6 us (89%)
  local copies, waits for them, and re-layouts  1.96 us (6%)
  other arithmetic  1.49 us (5%)
    pallas_call x1, Pallas kernels, per_device(): pl.pallas_call(functools.partial(fused, n_strip, n_sub), out_shape=jax.Sh...  28.6 us
    unnamed x3, local copies, waits for them, and re-layouts  1.87 us
    mul x1, other arithmetic, per_device(): key = box_of_patch.reshape(n_patch) * n_patch + ids  0.68 us

profile of v4, /device:TPU:1, one launch (start us, length us, event | category | flops | bytes accessed | tf_op | source)
XLA Modules:
  0.0 32.0 jit_solution(1031948593223558582)
XLA Ops:
  0.0 0.7 %broadcast_multiply_fusion = s32[4,16]{1,0:T(4,128)S(1)} fusion(s32[4,16]{1,0:T(4,128)} %param.12), kind=kLoop, calls=%fused_computation.3 | loop fusion | flops 64 | bytes 512 | tf_op jit(solution)/shard_map/mul | solution.py:482
  0.7 0.1 mul.19
  0.8 0.2 convert_reduce_fusion.slot_ref
  1.0 0.0 copy-start
  1.0 0.6 %select_reduce_fusion.perm_ref = s32[64]{0:T(128)} fusion(s32[64]{0:T(128)S(1)} %convert_reduce_fusion.slot_ref), kind=kLoop, calls=%fused_computation | loop fusion | flops 12224 | bytes 512 | tf_op jit(solution)/shard_map/reduce_sum | solution.py:484
  1.6 0.0 copy-done
  1.6 28.6 %shard_map.91 = bf16[64,32,128]{2,1,0:T(8,128)(2,1)} custom-call(s32[64]{0:T(128)} %select_reduce_fusion.perm_ref, s32[64]{0:T(128)} %copy-done, s32[9,4,16]{2,1,0:T(4,128)} %bitcast.10, bf16[4,16,32,128]{3,2,1,0:T(8,128)(2,1)} %cur_in.1, bf16[4,9,16,1024]{3,2,1,0:T(8,128)(2,1)} %bitcast.8, f32[64,128]{1,0:T(8,128)} %bitcast.9, ...), custom_call_target="tpu_custom_call" | custom-call | tf_op jit(solution)/shard_map/pallas_call | solution.py:529
  30.2 1.9 %copy.11 = bf16[4,16,32,128]{3,2,1,0:T(8,128)(2,1)} copy(bf16[4,16,32,128]{3,2,1,0:T(8,128)(2,1)} %bitcast.7) | data formatting | bytes 1048576
  (1 shorter events, 0.0 us)
Async XLA Ops:
  1.0 0.6 %copy-start = (s32[64]{0:T(128)}, s32[64]{0:T(128)S(1)}, u32[]{:S(2)}) copy-start(s32[64]{0:T(128)S(1)} %convert_reduce_fusion.slot_ref) | copy-start | bytes 772
